TPU v7x, 32 devices: a whole 2x2x4 slice. The times are simulated.
32 devices in a mesh: dev: 32 (over z, y, x, core).
Axes of the slice: x: 2, y: 2, z: 4, core: 2. Of those that a mesh axis runs over, the one named last changes fastest.
Arguments:
- diagonal: float32 [16384, 512], P('dev'), may hold values from -50 to 250, as said below
- panel: bfloat16 [98304, 512], P('dev'), may hold values from -3 to 3
- counts: int32 [32], P('dev'), may hold values from 1 to 6, 112 in all
- target_map: int32 [32, 21], P('dev'), may hold values from 0 to 7
- trailing: float32 [16384, 512], P('dev'), may hold values from -6 to 6
Outputs:
- diag_factor: float32 [16384, 512], P('dev')
- panel_factor: bfloat16 [98304, 512], P('dev')
- updated: float32 [16384, 512], P('dev')
- logdet_mean: float32 [], replicated
Inputs may be any that keep to these rules, and one draw needn't show every extreme that they name: Each block of 512 rows of diagonal is symmetric positive definite. `counts`: some supernode holds 6 panel blocks.
All inputs are finite; a program needn't handle non-finite values.
Results may differ from a plain program's by a relative error of at most 0.006.
Values may be sent and summed in bfloat16 or wider, within the bound.
A program may use at most 128 MiB of HBM per device.

v0:
```python
import jax
import jax.numpy as jnp
import numpy as np
from jax import lax
from jax.sharding import PartitionSpec as P

GROUP = 8


def from_partner(block, axis, distance):
    count = lax.axis_size(axis)
    route = []
    for low in range(count):
        high = low | 1 << distance
        if high != low and high < count:
            route += [(low, high), (high, low)]
    return lax.ppermute(block, axis, route)


def pair_tables(block_count):
    pair_rows = np.array([i for i in range(block_count) for j in range(i + 1)], dtype=np.int32)
    pair_cols = np.array([j for i in range(block_count) for j in range(i + 1)], dtype=np.int32)
    return (jnp.asarray(pair_rows), jnp.asarray(pair_cols))


def lookup(small_table, position):
    return jnp.sum(
        jnp.where(jnp.arange(small_table.shape[0], dtype=jnp.int32) == position, small_table, 0)
    )


def add_update(totals, source, row_block, col_block, target):
    block_width = source.shape[1]
    left_block = lax.dynamic_slice_in_dim(source, row_block * block_width, block_width, 0)
    right_block = lax.dynamic_slice_in_dim(source, col_block * block_width, block_width, 0)
    update = lax.dot_general(
        left_block, right_block, (((1,), (1,)), ((), ())), preferred_element_type=jnp.float32
    )
    current = lax.dynamic_slice_in_dim(totals, target, 1, 0)
    return lax.dynamic_update_slice_in_dim(totals, current - update[None], target, 0)


def local(diagonal, panel, counts, target_map, trailing):
    block_width = diagonal.shape[1]
    blocks = panel.shape[0] // block_width
    factor = jnp.linalg.cholesky(diagonal)
    solved = lax.linalg.triangular_solve(
        factor, panel.astype(jnp.float32), left_side=False, lower=True, transpose_a=True
    )
    block_of_row = jnp.arange(blocks * block_width, dtype=jnp.int32) // block_width
    panel_factor = jnp.where((block_of_row < counts[0])[:, None], solved, 0.0).astype(jnp.bfloat16)
    logterm = 2.0 * jnp.sum(jnp.log(jnp.diagonal(factor)))
    logdet_total = lax.psum(logterm, "dev")
    logdet_mean = logdet_total / (lax.axis_size("dev") * block_width)
    pair_rows, pair_cols = pair_tables(blocks)
    member = lax.axis_index("dev") % GROUP
    totals = jnp.zeros((GROUP, block_width, block_width), jnp.float32)
    live_tasks = counts[0] * (counts[0] + 1) // 2
    own_targets = target_map[0]

    def own_turn(position, totals):
        return add_update(
            totals,
            panel_factor,
            lookup(pair_rows, position),
            lookup(pair_cols, position),
            lookup(own_targets, position),
        )

    totals = lax.fori_loop(0, live_tasks, own_turn, totals)
    half_size = GROUP
    for bit_number in range(GROUP.bit_length() - 2, -1, -1):
        half_size = half_size // 2
        upper_bit = member // 2**bit_number % 2
        kept_half = lax.dynamic_slice_in_dim(totals, upper_bit * half_size, half_size, 0)
        sent_half = lax.dynamic_slice_in_dim(totals, (1 - upper_bit) * half_size, half_size, 0)
        totals = kept_half + from_partner(sent_half.astype(jnp.bfloat16), "dev", bit_number).astype(
            sent_half.dtype
        )
    updated = trailing + totals[0]
    return (factor, panel_factor, updated, logdet_mean)


def solution(mesh):
    return jax.shard_map(
        local,
        mesh=mesh,
        in_specs=(P("dev", None), P("dev", None), P("dev"), P("dev", None), P("dev", None)),
        out_specs=(P("dev", None), P("dev", None), P("dev", None), P()),
        check_vma=False,
    )
```

profile of v0, /device:TPU:0, one launch (start us, length us, event | category | flops | bytes accessed | tf_op | source)
XLA Modules:
  0.0 467.1 jit_solution(2068441298369070098)
XLA Ops:
  3.3 11.7 %cholesky.104 = f32[128,128]{1,0:T(8,128)S(1)} custom-call(f32[128,128]{1,0:T(8,128)S(1)} %cholesky.266), custom_call_target="Cholesky" | custom-call | tf_op jit(solution)/shard_map/jit(cholesky)/cholesky | solution.py:46
  15.2 9.8 %custom-call.30 = f32[1,128,128]{1,2,0:T(8,128)S(1)} custom-call(f32[1,128,128]{2,1,0:T(8,128)S(1)} %get-tuple-element.123), custom_call_target="InvertDiagBlocksLowerTriangular" | custom-call | tf_op jit(solution)/shard_map/jit(cholesky)/cholesky | solution.py:46
  25.6 11.7 %cholesky.217 = f32[128,128]{1,0:T(8,128)S(1)} custom-call(f32[128,128]{1,0:T(8,128)S(1)} %cholesky.270), custom_call_target="Cholesky" | custom-call | tf_op jit(solution)/shard_map/jit(cholesky)/cholesky | solution.py:46
  37.4 10.0 %custom-call.31 = f32[1,128,128]{1,2,0:T(8,128)S(1)} custom-call(f32[1,128,128]{2,1,0:T(8,128)S(1)} %get-tuple-element.120), custom_call_target="InvertDiagBlocksLowerTriangular" | custom-call | tf_op jit(solution)/shard_map/jit(cholesky)/cholesky | solution.py:46
  48.1 11.7 %cholesky.238 = f32[128,128]{1,0:T(8,128)S(1)} custom-call(f32[128,128]{1,0:T(8,128)S(1)} %cholesky.275), custom_call_target="Cholesky" | custom-call | tf_op jit(solution)/shard_map/jit(cholesky)/cholesky | solution.py:46
  59.9 9.8 %custom-call.32 = f32[1,128,128]{1,2,0:T(8,128)S(1)} custom-call(f32[1,128,128]{2,1,0:T(8,128)S(1)} %get-tuple-element.117), custom_call_target="InvertDiagBlocksLowerTriangular" | custom-call | tf_op jit(solution)/shard_map/jit(cholesky)/cholesky | solution.py:46
  70.3 11.7 %cholesky.255 = f32[128,128]{1,0:T(8,128)S(1)} custom-call(f32[128,128]{1,0:T(8,128)S(1)} %convolution_subtract_fusion.4), custom_call_target="Cholesky" | custom-call | tf_op jit(solution)/shard_map/jit(cholesky)/cholesky | solution.py:46
  86.5 11.5 %fusion.19 = (f32[512,512]{1,0:T(8,128)S(1)}, f32[512,512]{1,0:T(8,128)}) fusion(f32[512,512]{1,0:T(8,128)S(1)} %get-tuple-element.115, pred[]{:T(512)S(6)} %cholesky.260), kind=kLoop, calls=%fused_computation.42 | loop fusion | flops 1048576 | bytes 3145729 | tf_op jit(solution)/shard_map/triangular_solve | solution.py:47
  98.0 8.0 %while.12 = (s32[]{:T(128)}, f32[512,512]{1,0:T(8,128)S(1)}, s32[4,2]{0,1:T(2,128)S(1)}, f32[4,128,128]{2,1,0:T(8,128)S(1)}, s32[]{:T(128)}) while((s32[]{:T(128)}, f32[512,512]{1,0:T(8,128)S(1)}, s32[4,2]{0,1:T(2,128)S(1)}, f32[4,128,128]{2,1,0:T(8,128)S(1)}, s32[]{:T(128)}) %tuple.56), condition=%wide.while_cond, body=%wide.while_body.sunk | while | flops 2 | bytes 131189 | solution.py:47
  106.0 39.3 %custom-call.33 = f32[4,128,128]{1,2,0:T(8,128)S(1)} custom-call(f32[4,128,128]{2,1,0:T(8,128)S(1)} %get-tuple-element.50), custom_call_target="InvertDiagBlocksLowerTriangular" | custom-call | tf_op jit(solution)/shard_map/triangular_solve | solution.py:47
  145.3 2.8 convert_element_type.24
  154.4 5.3 %convolution_subtract_fusion.1 = f32[3072,128]{1,0:T(8,128)S(1)} fusion(f32[3072,128]{0,1:T(8,128)S(1)} %fusion.32, f32[3072,128]{0,1:T(8,128)S(1)} %bitcast.65, f32[3072,512]{1,0:T(8,128)S(1)} %convert_element_type.24, f32[512,512]{1,0:T(8,128)S(1)} %get-tuple-element.245), kind=kOutput, calls=%fused_computation.24 | convolution fusion | flops 1209139200 | bytes 6422528 | tf_op jit(solution)/shard_map/triangular_solve | solution.py:47
  161.2 8.2 %fusion.12 = f32[3072,128]{1,0:T(8,128)S(1)} fusion(f32[3072,128]{0,1:T(8,128)S(1)} %fusion.31, f32[3072,128]{0,1:T(8,128)S(1)} %fusion.32, f32[3072,128]{0,1:T(8,128)S(1)} %bitcast.66, f32[3072,512]{1,0:T(8,128)S(1)} %convert_element_type.24, f32[512,512]{1,0:T(8,128)S(1)} %get-tuple-element.245), kind=kOutput, calls=%fused_computation.25 | convolution fusion | flops 1814691840 | bytes 8060928 | tf_op jit(solution)/shard_map/triangular_solve | solution.py:47
  173.0 3.2 copy.16
  176.2 4.3 broadcast_in_dim.34
  180.5 7.4 %while.13 = (s32[]{:T(128)}, f32[8,512,512]{2,1,0:T(8,128)}, s32[]{:T(128)}, s32[21]{0:T(128)S(1)}, bf16[3072,512]{1,0:T(8,128)(2,1)S(1)}, /*index=5*/s32[]{:T(1...) while((s32[]{:T(128)}, f32[8,512,512]{2,1,0:T(8,128)}, ...), condition=%wide.region_12.13_spmd.clone, body=%wide.region_8.12_spmd.sunk.clone.sunk | while | flops 268697792 | bytes 3146263 | solution.py:70
  188.0 4.9 %dynamic-slice_convert_fusion = bf16[4,512,512]{2,1,0:T(8,128)(2,1)} fusion(f32[8,512,512]{2,1,0:T(8,128)} %get-tuple-element.42, s32[]{:T(128)S(6)} %select_n.98), kind=kLoop, calls=%fused_computation.22 | loop fusion | bytes 4194308 | tf_op jit(solution)/shard_map/convert_element_type | solution.py:77
  192.9 104.1 %collective-permute-start = (bf16[4,512,512]{2,1,0:T(8,128)(2,1)}, bf16[4,512,512]{2,1,0:T(8,128)(2,1)}, u32[]{:S(2)}, u32[]{:S(2)}) collective-permute-start(bf16[4,512,512]{2,1,0:T(8,128)(2,1)} %dynamic-slice_convert_fusion), channel_id=1, source_target_pairs={{0,4},{4,0},{1,5},{5,1},{2,6},{6,2},{3,7},{7,3},{8,12},{12,8},{9,1... | collective-permute-start | bytes 6291464 | tf_op jit(solution)/shard_map/ppermute | solution.py:17
  297.0 45.4 %collective-permute-done = bf16[4,512,512]{2,1,0:T(8,128)(2,1)} collective-permute-done((bf16[4,512,512]{2,1,0:T(8,128)(2,1)}, bf16[4,512,512]{2,1,0:T(8,128)(2,1)}, u32[]{:S(2)}, u32[]{:S(2)}) %collective-permute-start) | collective-permute-done | bytes 2097184 | tf_op jit(solution)/shard_map/ppermute | solution.py:17
  342.3 3.5 convert_add_fusion
  347.9 23.7 %collective-permute-start.1 = (bf16[2,512,512]{2,1,0:T(8,128)(2,1)S(1)}, bf16[2,512,512]{2,1,0:T(8,128)(2,1)}, u32[]{:S(2)}, u32[]{:S(2)}) collective-permute-start(bf16[2,512,512]{2,1,0:T(8,128)(2,1)S(1)} %dynamic-slice_convert_fusion.1), channel_id=1, source_target_pairs={{0,2},{2,0},{1,3},{3,1},{4,6},{6,4},{5,7},{7,5},{8,10},{10,8},{9,1... | collective-permute-start | bytes 3145736 | tf_op jit(solution)/shard_map/ppermute | solution.py:17
  371.6 12.9 %collective-permute-done.1 = bf16[2,512,512]{2,1,0:T(8,128)(2,1)} collective-permute-done((bf16[2,512,512]{2,1,0:T(8,128)(2,1)S(1)}, bf16[2,512,512]{2,1,0:T(8,128)(2,1)}, u32[]{:S(2)}, u32[]{:S(2)}) %collective-permute-start.1) | collective-permute-done | bytes 1048608 | tf_op jit(solution)/shard_map/ppermute | solution.py:17
  387.7 4.5 gather_fusion
  393.5 68.7 %psum.7 = f32[]{:T(128)} all-reduce(f32[]{:T(128)S(6)} %mul_shard_map.3), channel_id=1, replica_groups=mesh['dev'=32] {'dev'}, use_global_device_ids=true, to_apply=%region_14.15 | all-reduce | flops 1 | bytes 8 | tf_op jit(solution)/shard_map/psum | solution.py:53
  (66 shorter events, 37.5 us)
Async XLA Ops:
  0.6 2.4 copy-start.3
  176.2 4.3 copy-start.4
  176.2 4.3 copy-start.5
  176.2 4.3 copy-start.6
  188.0 4.9 %copy-start = (bf16[3072,512]{1,0:T(8,128)(2,1)}, bf16[3072,512]{1,0:T(8,128)(2,1)S(1)}, u32[]{:S(2)}) copy-start(bf16[3072,512]{1,0:T(8,128)(2,1)S(1)} %get-tuple-element.244) | copy-start | bytes 9437188
  192.9 149.4 %collective-permute-start = (bf16[4,512,512]{2,1,0:T(8,128)(2,1)}, bf16[4,512,512]{2,1,0:T(8,128)(2,1)}, u32[]{:S(2)}, u32[]{:S(2)}) collective-permute-start(bf16[4,512,512]{2,1,0:T(8,128)(2,1)} %dynamic-slice_convert_fusion), channel_id=1, source_target_pairs={{0,4},{4,0},{1,5},{5,1},{2,6},{6,2},{3,7},{7,3},{8,12},{12,8},{9,1... | collective-permute-start | bytes 6291464 | tf_op jit(solution)/shard_map/ppermute | solution.py:17
  345.9 1.9 copy-start.1
  347.9 36.6 %collective-permute-start.1 = (bf16[2,512,512]{2,1,0:T(8,128)(2,1)S(1)}, bf16[2,512,512]{2,1,0:T(8,128)(2,1)}, u32[]{:S(2)}, u32[]{:S(2)}) collective-permute-start(bf16[2,512,512]{2,1,0:T(8,128)(2,1)S(1)} %dynamic-slice_convert_fusion.1), channel_id=1, source_target_pairs={{0,2},{2,0},{1,3},{3,1},{4,6},{6,4},{5,7},{7,5},{8,10},{10,8},{9,1... | collective-permute-start | bytes 3145736 | tf_op jit(solution)/shard_map/ppermute | solution.py:17
  371.6 16.1 %copy-start.2 = (f32[512,512]{1,0:T(8,128)S(1)}, f32[512,512]{1,0:T(8,128)}, u32[]{:S(2)}) copy-start(f32[512,512]{1,0:T(8,128)} %get-tuple-element.109) | copy-start | bytes 3145732
  387.7 75.2 %collective-permute-start.2 = (bf16[1,512,512]{2,1,0:T(8,128)(2,1)}, bf16[1,512,512]{2,1,0:T(8,128)(2,1)}, u32[]{:S(2)}, u32[]{:S(2)}) collective-permute-start(bf16[1,512,512]{2,1,0:T(8,128)(2,1)} %dynamic-slice_convert_fusion.2), channel_id=1, source_target_pairs={{0,1},{1,0},{2,3},{3,2},{4,5},{5,4},{6,7},{7,6},{8,9},{9,8},{10,11... | collective-permute-start | bytes 1572872 | tf_op jit(solution)/shard_map/ppermute | solution.py:17
where the time goes:
time: 469 us; the launch traced here: 467 us
  other arithmetic  145 us (31%)
  starting transfers between devices  128 us (27%)
  blocking collectives  68.7 us (15%)
  waiting for transfers between devices  58.3 us (12%)
  local copies, waits for them, and re-layouts  29.5 us (6%)
  matrix products  27.3 us (6%)
  between operations  7.26 us (2%)
    ppermute x3, starting transfers between devices, from_partner(): return lax.ppermute(block, axis, route)  128 us
    another operation x14, other arithmetic, local(): factor = jnp.linalg.cholesky(diagonal)  78.6 us
    psum x1, blocking collectives, local(): logdet_total = lax.psum(logterm, 'dev')  68.7 us
    ppermute x3, waiting for transfers between devices, from_partner(): return lax.ppermute(block, axis, route)  58.3 us
    another operation x3, other arithmetic, local(): lax.linalg.triangular_solve(factor, panel.astype(jnp.float32), left_side=...  50.8 us
    another operation x7, matrix products, local(): lax.linalg.triangular_solve(factor, panel.astype(jnp.float32), left_side=...  22.7 us
  transfers between devices with their start and end apart: 3, of which 2 were waited for; matrix products, arithmetic and copies ran while one was open for 1% of the time, Pallas kernels for 0%

commit v1 on v0

v1 whole, which is shorter than its diff:
```python
import functools

import jax
import jax.numpy as jnp
from jax import lax
from jax.experimental import pallas as pl
from jax.experimental.pallas import tpu as pltpu
from jax.sharding import PartitionSpec as P

GROUP = 8
BASE = 128
STEP = 8
ROWS = 8


def dot_t(left, right, precision=None):
    return lax.dot_general(
        left, right, (((1,), (1,)), ((), ())), precision=precision, preferred_element_type=jnp.float32
    )


def factor_base(block):
    size = block.shape[0]
    shape = (ROWS, size)
    groups = size // ROWS
    sublane = lax.broadcasted_iota(jnp.int32, shape, 0)
    lane = lax.broadcasted_iota(jnp.int32, shape, 1)
    work = [block[g * ROWS : (g + 1) * ROWS, :] for g in range(groups)]
    side = [jnp.where(lane == sublane + g * ROWS, 1.0, 0.0).astype(jnp.float32) for g in range(groups)]
    upper, inverse = [None] * groups, [None] * groups
    for first in range(0, size, STEP):
        own, offset = first // ROWS, first % ROWS
        following = range((first + STEP) // ROWS, groups)
        columns = {
            g: [jnp.broadcast_to(work[g][:, first + j : first + j + 1], shape) for j in range(STEP)]
            for g in sorted({own, *following})
        }
        entry = {
            (i, j): jnp.broadcast_to(columns[own][j][offset + i : offset + i + 1, :], shape)
            for j in range(STEP)
            for i in range(j, STEP)
        }
        scale = []
        for j in range(STEP):
            scale.append(lax.rsqrt(entry[j, j]))
            for i in range(j + 1, STEP):
                entry[i, j] = entry[i, j] * scale[j]
            for i in range(j + 1, STEP):
                for m in range(j + 1, i + 1):
                    entry[i, m] = entry[i, m] - entry[i, j] * entry[m, j]
        rows, side_rows = [], []
        for j in range(STEP):
            row = jnp.broadcast_to(work[own][offset + j : offset + j + 1, :], shape)
            side_row = jnp.broadcast_to(side[own][offset + j : offset + j + 1, :], shape)
            for m in range(j):
                row = row - entry[j, m] * rows[m]
                side_row = side_row - entry[j, m] * side_rows[m]
            rows.append(row * scale[j])
            side_rows.append(side_row * scale[j])
        for j in range(STEP):
            at = sublane == offset + j
            upper[own] = rows[j] if upper[own] is None else jnp.where(at, rows[j], upper[own])
            inverse[own] = side_rows[j] if inverse[own] is None else jnp.where(at, side_rows[j], inverse[own])
        for g in following:
            lower = []
            for j in range(STEP):
                column = columns[g][j]
                for m in range(j):
                    column = column - lower[m] * entry[j, m]
                lower.append(column * scale[j])
            for j in range(STEP):
                work[g] = work[g] - lower[j] * rows[j]
                side[g] = side[g] - lower[j] * side_rows[j]
    return jnp.concatenate(upper, axis=0), jnp.concatenate(inverse, axis=0)


def factor_kernel(
    counts, targets, diagonal, panel, factor, solved, sums, logterm, work, inverse, high, low, totals
):
    width = diagonal.shape[0]
    blocks = panel.shape[0] // width
    steps = width // BASE
    exact = lax.Precision.HIGHEST
    work[...] = diagonal[...]
    factor[...] = jnp.zeros_like(factor)
    inverse[...] = jnp.zeros_like(inverse)
    totals[...] = jnp.zeros_like(totals)
    row = lax.broadcasted_iota(jnp.int32, (BASE, BASE), 0)
    col = lax.broadcasted_iota(jnp.int32, (BASE, BASE), 1)

    def eliminate(step, logs):
        here = pl.ds(pl.multiple_of(step * BASE, BASE), BASE)
        upper, inverted = factor_base(work[here, here])
        factor[here, here] = jnp.where(row >= col, upper.T, 0.0)
        inverse[here, here] = inverted
        for static in range(steps):

            @pl.when(step == static)
            def _():
                start, stop = static * BASE, (static + 1) * BASE
                own = inverse[start:stop, start:stop]
                if stop < width:
                    below = dot_t(work[stop:, start:stop], own, exact)
                    factor[stop:, start:stop] = below
                    work[stop:, stop:] -= dot_t(below, below, exact)
                if start > 0:
                    product = jnp.dot(
                        factor[start:stop, :start],
                        inverse[:start, :start],
                        precision=exact,
                        preferred_element_type=jnp.float32,
                    )
                    inverse[start:stop, :start] = -jnp.dot(
                        own, product, precision=exact, preferred_element_type=jnp.float32
                    )

        pivots = jnp.sum(jnp.where(row == col, upper, 0.0), axis=0, keepdims=True)
        return logs + jnp.log(pivots)

    logs = lax.fori_loop(0, steps, eliminate, jnp.zeros((1, BASE), jnp.float32))
    logterm[...] = jnp.broadcast_to(2.0 * jnp.sum(logs, axis=1, keepdims=True), logterm.shape)
    high[...] = inverse[...].astype(jnp.bfloat16)
    low[...] = (inverse[...] - high[...].astype(jnp.float32)).astype(jnp.bfloat16)
    live = counts[0]
    half = width // 2

    def solve(block, _):
        here = pl.ds(pl.multiple_of(block * width, width), width)

        @pl.when(block < live)
        def _():
            left = panel[here, :half]
            solved[here, :half] = (
                dot_t(left, high[:half, :half]) + dot_t(left, low[:half, :half])
            ).astype(jnp.bfloat16)
            left = panel[here, :]
            solved[here, half:] = (dot_t(left, high[half:, :]) + dot_t(left, low[half:, :])).astype(jnp.bfloat16)

        @pl.when(block >= live)
        def _():
            solved[here, :] = jnp.zeros((width, width), jnp.bfloat16)

        return 0

    lax.fori_loop(0, blocks, solve, 0)

    def update_row(i, _):
        left = pl.ds(pl.multiple_of(i * width, width), width)

        def update(j, _):
            right = pl.ds(pl.multiple_of(j * width, width), width)
            target = targets[0, i * (i + 1) // 2 + j]
            totals[target] += dot_t(solved[left, :], solved[right, :])
            return 0

        return lax.fori_loop(0, i + 1, update, 0)

    lax.fori_loop(0, live, update_row, 0)
    for target in range(GROUP):
        sums[target] = (-totals[target]).astype(sums.dtype)


def factor_and_update(diagonal, panel, counts, target_map):
    width = diagonal.shape[1]
    vmem = pl.BlockSpec(memory_space=pltpu.VMEM)
    smem = pl.BlockSpec(memory_space=pltpu.SMEM)
    return pl.pallas_call(
        factor_kernel,
        out_shape=(
            jax.ShapeDtypeStruct(diagonal.shape, jnp.float32),
            jax.ShapeDtypeStruct(panel.shape, jnp.bfloat16),
            jax.ShapeDtypeStruct((GROUP, width, width), jnp.bfloat16),
            jax.ShapeDtypeStruct((8, 128), jnp.float32),
        ),
        in_specs=[smem, smem, vmem, vmem],
        out_specs=(vmem, vmem, vmem, vmem),
        scratch_shapes=[
            pltpu.VMEM((width, width), jnp.float32),
            pltpu.VMEM((width, width), jnp.float32),
            pltpu.VMEM((width, width), jnp.bfloat16),
            pltpu.VMEM((width, width), jnp.bfloat16),
            pltpu.VMEM((GROUP, width, width), jnp.float32),
        ],
        compiler_params=pltpu.CompilerParams(vmem_limit_bytes=48 * 1024 * 1024),
        name="factor_and_update",
    )(counts, target_map, diagonal, panel)


def from_partner(block, axis, distance):
    count = lax.axis_size(axis)
    route = []
    for low in range(count):
        high = low | 1 << distance
        if high != low and high < count:
            route += [(low, high), (high, low)]
    return lax.ppermute(block, axis, route)


def local(diagonal, panel, counts, target_map, trailing):
    block_width = diagonal.shape[1]
    factor, panel_factor, totals, logterm = factor_and_update(diagonal, panel, counts, target_map)
    logdet_total = lax.psum(logterm[0, 0], "dev")
    logdet_mean = logdet_total / (lax.axis_size("dev") * block_width)
    member = lax.axis_index("dev") % GROUP
    half_size = GROUP
    totals = totals.reshape((2,) * (GROUP.bit_length() - 1) + totals.shape[1:])
    for bit_number in range(GROUP.bit_length() - 1):
        axis = totals.ndim - 3
        upper_bit = member // 2**bit_number % 2
        kept_half = lax.dynamic_index_in_dim(totals, upper_bit, axis, keepdims=False)
        sent_half = lax.dynamic_index_in_dim(totals, 1 - upper_bit, axis, keepdims=False)
        totals = kept_half.astype(jnp.float32) + from_partner(
            sent_half.astype(jnp.bfloat16), "dev", bit_number
        ).astype(jnp.float32)
    updated = trailing + totals
    return (factor, panel_factor, updated, logdet_mean)


def solution(mesh):
    return jax.shard_map(
        local,
        mesh=mesh,
        in_specs=(P("dev", None), P("dev", None), P("dev"), P("dev", None), P("dev", None)),
        out_specs=(P("dev", None), P("dev", None), P("dev", None), P()),
        check_vma=False,
    )
```

time: 469 us -> 141 us (0.30)
  other arithmetic: 145 us -> 6.92 us
  starting transfers between devices: 128 us -> 10.3 us
  Pallas kernels: 0 us -> 32.4 us
  waiting for transfers between devices: 58.3 us -> 27.9 us
  matrix products: 27.3 us -> 0 us
  blocking collectives: 68.7 us -> 49.2 us
  local copies, waits for them, and re-layouts: 29.5 us -> 11.2 us
    another operation x17 -> x0, other arithmetic: 129 us -> none  [the longest x14 78.6 us: local(): factor = jnp.linalg.cholesky(diagonal)]
    ppermute x3, starting transfers between devices: 128 us -> 10.3 us  [from_partner(): return lax.ppermute(block, axis, route)]
    pallas_call x0 -> x1, Pallas kernels: none -> 32.4 us  [factor_and_update(): pl.pallas_call(factor_kernel, out_shape=(jax.ShapeDtypeStruct(diagonal.sh...]
    ppermute x3, waiting for transfers between devices: 58.3 us -> 27.9 us  [from_partner(): return lax.ppermute(block, axis, route)]
    another operation x13 -> x0, matrix products: 24.6 us -> none  [the longest x7 22.7 us: local(): lax.linalg.triangular_solve(factor, panel.astype(jnp.float32), left_side=...]
    psum x1, blocking collectives: 68.7 us -> 49.2 us  [local(): logdet_total = lax.psum(logterm[0, 0], 'dev')]
    another operation x17 -> x0, local copies, waits for them, and re-layouts: 8.07 us -> none
    convert_element_type x3 -> x2, local copies, waits for them, and re-layouts: 5.89 us -> 1 us  [local(): sent_half.astype(jnp.bfloat16)]
  transfers between devices with their start and end apart: 3 -> 3, of which waited for: 2 -> 2; matrix products, arithmetic and copies ran while one was open for 1% -> 0% of each run, Pallas kernels for 0% -> 0%
where the time goes in v1:
time: 141 us
  blocking collectives  49.2 us (35%)
  Pallas kernels  32.4 us (23%)
  waiting for transfers between devices  27.9 us (20%)
  local copies, waits for them, and re-layouts  11.2 us (8%)
  starting transfers between devices  10.3 us (7%)
  other arithmetic  6.92 us (5%)
  between operations  3.16 us (2%)
    psum x1, blocking collectives, local(): logdet_total = lax.psum(logterm[0, 0], 'dev')  49.2 us
    pallas_call x1, Pallas kernels, factor_and_update(): pl.pallas_call(factor_kernel, out_shape=(jax.ShapeDtypeStruct(diagonal.sh...  32.4 us
    ppermute x3, waiting for transfers between devices, from_partner(): return lax.ppermute(block, axis, route)  27.9 us
    ppermute x3, starting transfers between devices, from_partner(): return lax.ppermute(block, axis, route)  10.3 us
    unnamed x10, local copies, waits for them, and re-layouts  5.7 us
    add x2, other arithmetic, local(): kept_half.astype(jnp.float32)  4.6 us
  transfers between devices with their start and end apart: 3, of which 2 were waited for; matrix products, arithmetic and copies ran while one was open for 0% of the time, Pallas kernels for 0%

profile of v1, /device:TPU:0, one launch (start us, length us, event | category | flops | bytes accessed | tf_op | source)
XLA Modules:
  0.0 141.1 jit_solution(15085515854181091805)
XLA Ops:
  1.3 0.0 copy-start
  1.3 1.9 %copy-done = bf16[3072,512]{1,0:T(8,128)(2,1)S(1)} copy-done((bf16[3072,512]{1,0:T(8,128)(2,1)S(1)}, bf16[3072,512]{1,0:T(8,128)(2,1)}, u32[]{:S(2)}) %copy-start) | copy-done | bytes 3145752
  3.2 0.0 copy-start.1
  3.2 1.2 copy-done.1
  4.4 0.7 copy-done.2
  5.1 32.4 %factor_and_update.1 = (f32[512,512]{1,0:T(8,128)}, bf16[3072,512]{1,0:T(8,128)(2,1)}, bf16[8,512,512]{2,1,0:T(8,128)(2,1)}, f32[8,128]{1,0:T(8,128)S(1)}) custom-call(s32[1]{0:T(128)S(6)} %copy.17.counts, s32[1,21]{1,0:T(1,128)S(1)} %copy-done.2, f32[512,512]{1,0:T(8,128)S(1)} %copy-done.1, bf16[3072,512]{1,0:T(8,128)(2,1)S(1)} %copy-done), custom_call_target="tpu_custom_call" | custom-call | tf_op jit(solution)/shard_map/factor_and_update/pallas_call | solution.py:167
  37.5 2.5 %constant_dynamic-slice_fusion.1 = (bf16[2,2,1,512,512]{4,3,2,1,0:T(8,128)(2,1)S(1)}, bf16[2,2,1,512,512]{4,3,2,1,0:T(8,128)(2,1)S(1)}) fusion(bf16[2,2,2,512,512]{4,3,2,1,0:T(8,128)(2,1)} %bitcast.20, s32[]{:T(128)S(6)} %select_n.50, s32[]{:T(128)S(6)} %select_n.51), kind=kLoop, calls=%fused_computation.11 | loop fusion | bytes 8388616 | tf_op jit(solution)/shard_map/jit(dynamic_index_in_dim)/dynamic_slice | solution.py:210
  40.0 1.5 %copy.16 = bf16[2,2,1,512,512]{4,3,0,1,2:T(8,128)(2,1)} copy(bf16[2,2,1,512,512]{4,3,2,1,0:T(8,128)(2,1)S(1)} %get-tuple-element.13) | data formatting | bytes 4194304 | tf_op jit(solution)/shard_map/jit(dynamic_index_in_dim)/dynamic_slice | solution.py:211
  41.4 2.9 %collective-permute-start = (bf16[2,2,512,512]{3,2,0,1:T(8,128)(2,1)}, bf16[2,2,512,512]{3,2,0,1:T(8,128)(2,1)}, u32[]{:S(2)}, u32[]{:S(2)}) collective-permute-start(bf16[2,2,512,512]{3,2,0,1:T(8,128)(2,1)} %bitcast.19), channel_id=1, source_target_pairs={{0,1},{1,0},{2,3},{3,2},{4,5},{5,4},{6,7},{7,6},{8,9},{9,8},{10,11... | collective-permute-start | bytes 6291464 | tf_op jit(solution)/shard_map/ppermute | solution.py:196
  44.4 4.1 %collective-permute-done = bf16[2,2,512,512]{3,2,0,1:T(8,128)(2,1)} collective-permute-done((bf16[2,2,512,512]{3,2,0,1:T(8,128)(2,1)}, bf16[2,2,512,512]{3,2,0,1:T(8,128)(2,1)}, u32[]{:S(2)}, u32[]{:S(2)}) %collective-permute-start) | collective-permute-done | bytes 2097184 | tf_op jit(solution)/shard_map/ppermute | solution.py:196
  48.5 2.3 %convert_add_fusion = f32[2,2,512,512]{3,2,0,1:T(8,128)S(1)} fusion(bf16[2,2,512,512]{3,2,0,1:T(8,128)(2,1)} %collective-permute-done, bf16[2,2,1,512,512]{4,3,2,1,0:T(8,128)(2,1)S(1)} %get-tuple-element.12), kind=kLoop, calls=%fused_computation | loop fusion | flops 3145728 | bytes 8388608 | tf_op jit(solution)/shard_map/add | solution.py:212
  50.8 0.0 copy-start.3
  50.8 1.9 %copy-done.3 = f32[2,2,512,512]{3,2,0,1:T(8,128)} copy-done((f32[2,2,512,512]{3,2,0,1:T(8,128)}, f32[2,2,512,512]{3,2,0,1:T(8,128)S(1)}, u32[]{:S(2)}) %copy-start.3) | copy-done | bytes 4194328
  52.7 0.1 fusion
  52.9 2.4 %collective-permute-start.1 = (bf16[2,512,512]{2,1,0:T(8,128)(2,1)S(1)}, bf16[2,512,512]{2,1,0:T(8,128)(2,1)}, u32[]{:S(2)}, u32[]{:S(2)}) collective-permute-start(bf16[2,512,512]{2,1,0:T(8,128)(2,1)S(1)} %fusion), channel_id=1, source_target_pairs={{0,2},{2,0},{1,3},{3,1},{4,6},{6,4},{5,7},{7,5},{8,10},{10,8},{9,1... | collective-permute-start | bytes 3145736 | tf_op jit(solution)/shard_map/ppermute | solution.py:196
  55.3 23.8 %collective-permute-done.1 = bf16[2,512,512]{2,1,0:T(8,128)(2,1)} collective-permute-done((bf16[2,512,512]{2,1,0:T(8,128)(2,1)S(1)}, bf16[2,512,512]{2,1,0:T(8,128)(2,1)}, u32[]{:S(2)}, u32[]{:S(2)}) %collective-permute-start.1) | collective-permute-done | bytes 1048608 | tf_op jit(solution)/shard_map/ppermute | solution.py:196
  79.1 2.3 %bitcast_add_fusion = f32[2,512,512]{2,1,0:T(8,128)S(1)} fusion(bf16[2,512,512]{2,1,0:T(8,128)(2,1)} %collective-permute-done.1, f32[2,2,512,512]{3,2,0,1:T(8,128)} %copy-done.3, s32[]{:T(128)S(6)} %select_n.54), kind=kLoop, calls=%fused_computation.2 | loop fusion | flops 1048576 | bytes 5242884 | tf_op jit(solution)/shard_map/add | solution.py:212
  81.4 0.9 fusion.2
  82.2 5.0 %collective-permute-start.2 = (bf16[512,512]{1,0:T(8,128)(2,1)}, bf16[512,512]{1,0:T(8,128)(2,1)}, u32[]{:S(2)}, u32[]{:S(2)}) collective-permute-start(bf16[512,512]{1,0:T(8,128)(2,1)} %fusion.2), channel_id=1, source_target_pairs={{0,4},{4,0},{1,5},{5,1},{2,6},{6,2},{3,7},{7,3},{8,12},{12,8},{9,1... | collective-permute-start | bytes 1572872 | tf_op jit(solution)/shard_map/ppermute | solution.py:196
  87.2 0.5 slice.3
  87.7 49.2 %psum.7 = f32[]{:T(128)} all-reduce(f32[]{:T(128)} %bitcast.7), channel_id=1, replica_groups=mesh['dev'=32] {'dev'}, use_global_device_ids=true, to_apply=%region_0.0 | all-reduce | flops 1 | bytes 8 | tf_op jit(solution)/shard_map/psum | solution.py:202
  137.6 0.0 collective-permute-done.2
  137.6 0.0 copy-done.4
  137.7 2.3 %fusion.1 = f32[512,512]{1,0:T(8,128)} fusion(f32[512,512]{1,0:T(8,128)S(1)} %copy-done.4, bf16[512,512]{1,0:T(8,128)(2,1)} %collective-permute-done.2, f32[2,512,512]{2,1,0:T(8,128)S(1)} %bitcast_add_fusion, s32[]{:T(128)S(6)} %select_n.58), kind=kLoop, calls=%fused_computation.7 | loop fusion | flops 786432 | bytes 3670020 | tf_op jit(solution)/shard_map/add | solution.py:215
  (2 shorter events, 0.0 us)
Async XLA Ops:
  1.3 1.9 %copy-start = (bf16[3072,512]{1,0:T(8,128)(2,1)S(1)}, bf16[3072,512]{1,0:T(8,128)(2,1)}, u32[]{:S(2)}) copy-start(bf16[3072,512]{1,0:T(8,128)(2,1)} %panel.1) | copy-start | bytes 9437188
  3.2 1.2 copy-start.1
  4.4 0.7 copy-start.2
  41.4 7.0 %collective-permute-start = (bf16[2,2,512,512]{3,2,0,1:T(8,128)(2,1)}, bf16[2,2,512,512]{3,2,0,1:T(8,128)(2,1)}, u32[]{:S(2)}, u32[]{:S(2)}) collective-permute-start(bf16[2,2,512,512]{3,2,0,1:T(8,128)(2,1)} %bitcast.19), channel_id=1, source_target_pairs={{0,1},{1,0},{2,3},{3,2},{4,5},{5,4},{6,7},{7,6},{8,9},{9,8},{10,11... | collective-permute-start | bytes 6291464 | tf_op jit(solution)/shard_map/ppermute | solution.py:196
  50.8 1.9 %copy-start.3 = (f32[2,2,512,512]{3,2,0,1:T(8,128)}, f32[2,2,512,512]{3,2,0,1:T(8,128)S(1)}, u32[]{:S(2)}) copy-start(f32[2,2,512,512]{3,2,0,1:T(8,128)S(1)} %convert_add_fusion) | copy-start | bytes 12582916
  52.9 26.2 %collective-permute-start.1 = (bf16[2,512,512]{2,1,0:T(8,128)(2,1)S(1)}, bf16[2,512,512]{2,1,0:T(8,128)(2,1)}, u32[]{:S(2)}, u32[]{:S(2)}) collective-permute-start(bf16[2,512,512]{2,1,0:T(8,128)(2,1)S(1)} %fusion), channel_id=1, source_target_pairs={{0,2},{2,0},{1,3},{3,1},{4,6},{6,4},{5,7},{7,5},{8,10},{10,8},{9,1... | collective-permute-start | bytes 3145736 | tf_op jit(solution)/shard_map/ppermute | solution.py:196
  55.3 82.4 %copy-start.4 = (f32[512,512]{1,0:T(8,128)S(1)}, f32[512,512]{1,0:T(8,128)}, u32[]{:S(2)}) copy-start(f32[512,512]{1,0:T(8,128)} %param.9) | copy-start | bytes 3145732
  82.2 55.4 %collective-permute-start.2 = (bf16[512,512]{1,0:T(8,128)(2,1)}, bf16[512,512]{1,0:T(8,128)(2,1)}, u32[]{:S(2)}, u32[]{:S(2)}) collective-permute-start(bf16[512,512]{1,0:T(8,128)(2,1)} %fusion.2), channel_id=1, source_target_pairs={{0,4},{4,0},{1,5},{5,1},{2,6},{6,2},{3,7},{7,3},{8,12},{12,8},{9,1... | collective-permute-start | bytes 1572872 | tf_op jit(solution)/shard_map/ppermute | solution.py:196

commit v2 on v1

--- a/solution.py
+++ b/solution.py
@@ -75,10 +75,32 @@
 
 
 def factor_kernel(
-    counts, targets, diagonal, panel, factor, solved, sums, logterm, work, inverse, high, low, totals
+    counts,
+    targets,
+    diagonal,
+    panel_source,
+    factor_result,
+    solved_result,
+    sums_result,
+    logterm,
+    work,
+    inverse,
+    high,
+    low,
+    totals,
+    factor,
+    panel,
+    solved,
+    panel_sem,
+    factor_sem,
+    solved_sem,
+    sums,
+    sums_sem,
 ):
     width = diagonal.shape[0]
     blocks = panel.shape[0] // width
+    fetch = pltpu.make_async_copy(panel_source, panel, panel_sem)
+    fetch.start()
     steps = width // BASE
     exact = lax.Precision.HIGHEST
     work[...] = diagonal[...]
@@ -118,9 +140,12 @@
         return logs + jnp.log(pivots)
 
     logs = lax.fori_loop(0, steps, eliminate, jnp.zeros((1, BASE), jnp.float32))
+    store_factor = pltpu.make_async_copy(factor, factor_result, factor_sem)
+    store_factor.start()
     logterm[...] = jnp.broadcast_to(2.0 * jnp.sum(logs, axis=1, keepdims=True), logterm.shape)
     high[...] = inverse[...].astype(jnp.bfloat16)
     low[...] = (inverse[...] - high[...].astype(jnp.float32)).astype(jnp.bfloat16)
+    fetch.wait()
     live = counts[0]
     half = width // 2
 
@@ -143,6 +168,8 @@
         return 0
 
     lax.fori_loop(0, blocks, solve, 0)
+    store_solved = pltpu.make_async_copy(solved, solved_result, solved_sem)
+    store_solved.start()
 
     def update_row(i, _):
         left = pl.ds(pl.multiple_of(i * width, width), width)
@@ -156,14 +183,23 @@
         return lax.fori_loop(0, i + 1, update, 0)
 
     lax.fori_loop(0, live, update_row, 0)
+    stores = []
     for target in range(GROUP):
         sums[target] = (-totals[target]).astype(sums.dtype)
+        store = pltpu.make_async_copy(sums.at[target], sums_result.at[target], sums_sem.at[target])
+        store.start()
+        stores.append(store)
+    for store in stores:
+        store.wait()
+    store_factor.wait()
+    store_solved.wait()
 
 
 def factor_and_update(diagonal, panel, counts, target_map):
     width = diagonal.shape[1]
     vmem = pl.BlockSpec(memory_space=pltpu.VMEM)
     smem = pl.BlockSpec(memory_space=pltpu.SMEM)
+    hbm = pl.BlockSpec(memory_space=pltpu.HBM)
     return pl.pallas_call(
         factor_kernel,
         out_shape=(
@@ -172,48 +208,200 @@
             jax.ShapeDtypeStruct((GROUP, width, width), jnp.bfloat16),
             jax.ShapeDtypeStruct((8, 128), jnp.float32),
         ),
-        in_specs=[smem, smem, vmem, vmem],
-        out_specs=(vmem, vmem, vmem, vmem),
+        in_specs=[smem, smem, vmem, hbm],
+        out_specs=(hbm, hbm, hbm, vmem),
         scratch_shapes=[
             pltpu.VMEM((width, width), jnp.float32),
             pltpu.VMEM((width, width), jnp.float32),
             pltpu.VMEM((width, width), jnp.bfloat16),
             pltpu.VMEM((width, width), jnp.bfloat16),
             pltpu.VMEM((GROUP, width, width), jnp.float32),
+            pltpu.VMEM(diagonal.shape, jnp.float32),
+            pltpu.VMEM(panel.shape, jnp.bfloat16),
+            pltpu.VMEM(panel.shape, jnp.bfloat16),
+            pltpu.SemaphoreType.DMA,
+            pltpu.SemaphoreType.DMA,
+            pltpu.SemaphoreType.DMA,
+            pltpu.VMEM((GROUP, width, width), jnp.bfloat16),
+            pltpu.SemaphoreType.DMA((GROUP,)),
         ],
-        compiler_params=pltpu.CompilerParams(vmem_limit_bytes=48 * 1024 * 1024),
+        compiler_params=pltpu.CompilerParams(vmem_limit_bytes=60 * 1024 * 1024),
         name="factor_and_update",
     )(counts, target_map, diagonal, panel)
 
 
-def from_partner(block, axis, distance):
-    count = lax.axis_size(axis)
-    route = []
-    for low in range(count):
-        high = low | 1 << distance
-        if high != low and high < count:
-            route += [(low, high), (high, low)]
-    return lax.ppermute(block, axis, route)
+def exchange_kernel(
+    count,
+    share,
+    sums,
+    logterm,
+    trailing,
+    updated,
+    logdet,
+    kept,
+    landed,
+    partial,
+    cross,
+    last,
+    second,
+    logs,
+    logs_landed,
+    local_sem,
+    core_send,
+    core_recv,
+    cross_send,
+    cross_recv,
+    last_send,
+    last_recv,
+    log_send,
+    log_recv,
+):
+    me = lax.axis_index("dev")
+    width = updated.shape[0]
+    half = width // 2
+    core, x, y = me % 2, me // 2 % 2, me // 4 % 2
+    bits = count.bit_length() - 1
+
+    def partner(bit):
+        return me + (1 - 2 * (me // 2**bit % 2)) * 2**bit
+
+    def remote(source, target, send, recv, bit):
+        return pltpu.make_async_remote_copy(
+            src_ref=source,
+            dst_ref=target,
+            send_sem=send,
+            recv_sem=recv,
+            device_id=(partner(bit),),
+            device_id_type=pl.DeviceIdType.MESH,
+        )
+
+    barrier = pltpu.get_barrier_semaphore()
+    for bit in range(bits):
+        pl.semaphore_signal(
+            barrier, inc=1, device_id=(partner(bit),), device_id_type=pl.DeviceIdType.MESH
+        )
+    local_copies, core_copies = [], []
+    places = [(1 - y, 1 - x), (y, 1 - x), (1 - y, x), (y, x)]
+    for n, (to_y, to_x) in enumerate(places):
+        copy = pltpu.make_async_copy(sums.at[to_y * 4 + to_x * 2 + core], kept.at[n], local_sem.at[n])
+        copy.start()
+        local_copies.append(copy)
+    logs[0] = logterm[...]
+    pl.semaphore_wait(barrier, bits)
+
+    order = [1, 2, 0, *range(3, bits)]
+    log_copies = []
+
+    def start_log(step):
+        copy = remote(logs.at[step], logs_landed.at[step], log_send.at[step], log_recv.at[step], order[step])
+        copy.start()
+        log_copies.append(copy)
+
+    def advance_log():
+        step = len(log_copies) - 1
+        if step < bits:
+            log_copies[step].wait()
+            logs[step + 1] = logs[step] + logs_landed[step]
+            if step + 1 < bits:
+                start_log(step + 1)
+            else:
+                log_copies.append(None)
+
+    start_log(0)
+    for n, (to_y, to_x) in enumerate(places):
+        copy = remote(
+            sums.at[to_y * 4 + to_x * 2 + 1 - core], landed.at[n], core_send.at[n], core_recv.at[n], 0
+        )
+        copy.start()
+        core_copies.append(copy)
+    upper, lower = pl.ds(0, half), pl.ds(half, half)
+    x_copies = [
+        remote(partial.at[n, upper], cross.at[n, upper], cross_send.at[n], cross_recv.at[n], 1)
+        for n in range(2)
+    ]
+    y_copies = [
+        remote(partial.at[2 * n, lower], cross.at[n, lower], cross_send.at[2 + n], cross_recv.at[2 + n], 2)
+        for n in range(2)
+    ]
+    for n in range(4):
+        local_copies[n].wait()
+        core_copies[n].wait_recv()
+        total = kept[n].astype(jnp.float32) + landed[n].astype(jnp.float32)
+        if n < 3:
+            partial[n] = total.astype(jnp.bfloat16)
+        else:
+            updated[...] = trailing[...] + total
+        if n < 2:
+            x_copies[n].start()
+        if n == 0 or n == 2:
+            y_copies[n // 2].start()
+        advance_log()
+    last_copies = []
+    for at, own, copies, bit, n in ((upper, 2, x_copies, 2, 0), (lower, 1, y_copies, 1, 1)):
+        copies[0].wait_recv()
+        total = partial[own, at, :].astype(jnp.float32) + cross[0, at, :].astype(jnp.float32)
+        second[at, :] = total.astype(jnp.bfloat16)
+        copy = remote(second.at[at], last.at[at], last_send.at[n], last_recv.at[n], bit)
+        copy.start()
+        last_copies.append(copy)
+    while len(log_copies) <= bits:
+        advance_log()
+    logdet[...] = logs[bits] * share
+    for at, copies, n in ((upper, x_copies, 0), (lower, y_copies, 1)):
+        copies[1].wait_recv()
+        updated[at, :] += cross[1, at, :].astype(jnp.float32)
+    for at, n in ((upper, 0), (lower, 1)):
+        last_copies[n].wait_recv()
+        updated[at, :] += last[at, :].astype(jnp.float32)
+    for copy in core_copies + x_copies + y_copies + last_copies:
+        copy.wait_send()
+
+
+def exchange(sums, logterm, trailing):
+    width = trailing.shape[1]
+    count = lax.axis_size("dev")
+    bits = count.bit_length() - 1
+    vmem = pl.BlockSpec(memory_space=pltpu.VMEM)
+    block = (width, width)
+    dma = pltpu.SemaphoreType.DMA
+    return pl.pallas_call(
+        functools.partial(exchange_kernel, count, 1.0 / (count * width)),
+        out_shape=(
+            jax.ShapeDtypeStruct(trailing.shape, jnp.float32),
+            jax.ShapeDtypeStruct(logterm.shape, jnp.float32),
+        ),
+        in_specs=[pl.BlockSpec(memory_space=pl.ANY), vmem, vmem],
+        out_specs=(vmem, vmem),
+        scratch_shapes=[
+            pltpu.VMEM((4, *block), jnp.bfloat16),
+            pltpu.VMEM((4, *block), jnp.bfloat16),
+            pltpu.VMEM((3, *block), jnp.bfloat16),
+            pltpu.VMEM((2, *block), jnp.bfloat16),
+            pltpu.VMEM(block, jnp.bfloat16),
+            pltpu.VMEM(block, jnp.bfloat16),
+            pltpu.VMEM((bits + 1, *logterm.shape), jnp.float32),
+            pltpu.VMEM((bits, *logterm.shape), jnp.float32),
+            dma((4,)),
+            dma((4,)),
+            dma((4,)),
+            dma((4,)),
+            dma((4,)),
+            dma((2,)),
+            dma((2,)),
+            dma((bits,)),
+            dma((bits,)),
+        ],
+        compiler_params=pltpu.CompilerParams(
+            collective_id=0, has_side_effects=True, vmem_limit_bytes=60 * 1024 * 1024
+        ),
+        name="exchange",
+    )(sums, logterm, trailing)
 
 
 def local(diagonal, panel, counts, target_map, trailing):
-    block_width = diagonal.shape[1]
-    factor, panel_factor, totals, logterm = factor_and_update(diagonal, panel, counts, target_map)
-    logdet_total = lax.psum(logterm[0, 0], "dev")
-    logdet_mean = logdet_total / (lax.axis_size("dev") * block_width)
-    member = lax.axis_index("dev") % GROUP
-    half_size = GROUP
-    totals = totals.reshape((2,) * (GROUP.bit_length() - 1) + totals.shape[1:])
-    for bit_number in range(GROUP.bit_length() - 1):
-        axis = totals.ndim - 3
-        upper_bit = member // 2**bit_number % 2
-        kept_half = lax.dynamic_index_in_dim(totals, upper_bit, axis, keepdims=False)
-        sent_half = lax.dynamic_index_in_dim(totals, 1 - upper_bit, axis, keepdims=False)
-        totals = kept_half.astype(jnp.float32) + from_partner(
-            sent_half.astype(jnp.bfloat16), "dev", bit_number
-        ).astype(jnp.float32)
-    updated = trailing + totals
-    return (factor, panel_factor, updated, logdet_mean)
+    factor, panel_factor, sums, logterm = factor_and_update(diagonal, panel, counts, target_map)
+    updated, logdet = exchange(sums, logterm, trailing)
+    return (factor, panel_factor, updated, logdet[0, 0])
 
 
 def solution(mesh):

time: 141 us -> 73.3 us (0.52); the launches traced: 141 us -> 72 us
  blocking collectives: 49.2 us -> 0 us
  Pallas kernels: 32.4 us -> 67.2 us
  waiting for transfers between devices: 27.9 us -> 0 us
  starting transfers between devices: 10.3 us -> 0 us
  local copies, waits for them, and re-layouts: 11.2 us -> 3.45 us
  other arithmetic: 6.92 us -> 0 us
  between operations: 3.16 us -> 1.29 us
    psum x1 -> x0, blocking collectives: 49.2 us -> none  [local(): logdet_total = lax.psum(logterm[0, 0], 'dev')]
    pallas_call x0 -> x1, Pallas kernels: none -> 35.2 us  [exchange(): pl.pallas_call(functools.partial(exchange_kernel, count, 1.0 / (count * w...]
    ppermute x3 -> x0, waiting for transfers between devices: 27.9 us -> none  [from_partner(): return lax.ppermute(block, axis, route)]
    ppermute x3 -> x0, starting transfers between devices: 10.3 us -> none  [from_partner(): return lax.ppermute(block, axis, route)]
    add x3 -> x0, other arithmetic: 6.92 us -> none  [the longest x2 4.6 us: local(): kept_half.astype(jnp.float32)]
    dynamic_slice x2 -> x0, local copies, waits for them, and re-layouts: 3.98 us -> none  [the longest x1 2.49 us: local(): lax.dynamic_index_in_dim(totals, upper_bit, axis, keepdims=False)]
    unnamed x10 -> x1, local copies, waits for them, and re-layouts: 5.7 us -> 2.26 us
  transfers between devices with their start and end apart: 3 -> 0, of which waited for: 2 -> 0; matrix products, arithmetic and copies ran while one was open for 0% -> 0% of each run, Pallas kernels for 0% -> 0%
where the time goes in v2:
time: 73.3 us; the launch traced here: 72 us
  Pallas kernels  67.2 us (92%)
  local copies, waits for them, and re-layouts  3.45 us (5%)
  between operations  1.29 us (2%)
    pallas_call x1, Pallas kernels, exchange(): pl.pallas_call(functools.partial(exchange_kernel, count, 1.0 / (count * w...  35.2 us
    pallas_call x1, Pallas kernels, factor_and_update(): pl.pallas_call(factor_kernel, out_shape=(jax.ShapeDtypeStruct(diagonal.sh...  32 us
    unnamed x1, local copies, waits for them, and re-layouts  2.26 us

profile of v2, /device:TPU:0, one launch (start us, length us, event | category | flops | bytes accessed | tf_op | source)
XLA Modules:
  0.0 72.0 jit_solution(3917122089170024720)
XLA Ops:
  1.3 32.0 %factor_and_update.1 = (f32[512,512]{1,0:T(8,128)}, bf16[3072,512]{1,0:T(8,128)(2,1)}, bf16[8,512,512]{2,1,0:T(8,128)(2,1)}, f32[8,128]{1,0:T(8,128)}) custom-call(s32[1]{0:T(128)S(6)} %copy.10.counts, s32[1,21]{1,0:T(1,128)} %targets.1, f32[512,512]{1,0:T(8,128)} %diagonal.1, bf16[3072,512]{1,0:T(8,128)(2,1)} %panel_source.1), custom_call_target="tpu_custom_call" | custom-call | tf_op jit(solution)/shard_map/factor_and_update/pallas_call | solution.py:203
  33.3 35.2 %exchange.1 = (f32[512,512]{1,0:T(8,128)}, f32[8,128]{1,0:T(8,128)}) custom-call(bf16[8,512,512]{2,1,0:T(8,128)(2,1)} %get-tuple-element.12.sums, f32[8,128]{1,0:T(8,128)} %get-tuple-element.13.logterm, f32[512,512]{1,0:T(8,128)} %trailing.1), custom_call_target="tpu_custom_call" | custom-call | tf_op jit(solution)/shard_map/exchange/pallas_call | solution.py:367
  68.5 1.2 %slice.3 = f32[1,1]{1,0:T(1,128)} slice(f32[8,128]{1,0:T(8,128)} %get-tuple-element.15), slice={[0:1], [0:1]} | slice | bytes 8 | tf_op jit(solution)/shard_map/slice | solution.py:404
  69.7 2.3 %copy.11 = f32[512,512]{1,0:T(8,128)} copy(f32[512,512]{1,0:T(8,128)} %get-tuple-element.22) | data formatting | bytes 2097152

commit v3 on v2

--- a/solution.py
+++ b/solution.py
@@ -11,6 +11,7 @@
 BASE = 128
 STEP = 8
 ROWS = 8
+ROOM = 8
 
 
 def dot_t(left, right, precision=None):
@@ -106,12 +107,13 @@
     work[...] = diagonal[...]
     factor[...] = jnp.zeros_like(factor)
     inverse[...] = jnp.zeros_like(inverse)
-    totals[...] = jnp.zeros_like(totals)
     row = lax.broadcasted_iota(jnp.int32, (BASE, BASE), 0)
     col = lax.broadcasted_iota(jnp.int32, (BASE, BASE), 1)
 
     def eliminate(step, logs):
         here = pl.ds(pl.multiple_of(step * BASE, BASE), BASE)
+        for extra in range(GROUP // steps):
+            totals[step * (GROUP // steps) + extra] = jnp.zeros((width, width), jnp.float32)
         upper, inverted = factor_base(work[here, here])
         factor[here, here] = jnp.where(row >= col, upper.T, 0.0)
         inverse[here, here] = inverted
@@ -171,18 +173,21 @@
     store_solved = pltpu.make_async_copy(solved, solved_result, solved_sem)
     store_solved.start()
 
-    def update_row(i, _):
-        left = pl.ds(pl.multiple_of(i * width, width), width)
-
-        def update(j, _):
+    def update(first, many):
+        found = []
+        for pair in [first + n for n in range(many)]:
+            i = sum((pair >= r * (r + 1) // 2).astype(jnp.int32) for r in range(1, blocks))
+            j = pair - i * (i + 1) // 2
+            left = pl.ds(pl.multiple_of(i * width, width), width)
             right = pl.ds(pl.multiple_of(j * width, width), width)
-            target = targets[0, i * (i + 1) // 2 + j]
-            totals[target] += dot_t(solved[left, :], solved[right, :])
-            return 0
-
-        return lax.fori_loop(0, i + 1, update, 0)
-
-    lax.fori_loop(0, live, update_row, 0)
+            found.append((targets[0, pair], dot_t(solved[left, :], solved[right, :])))
+        for target, product in found:
+            totals[target] += product
+        return 0
+
+    pairs = live * (live + 1) // 2
+    lax.fori_loop(0, pairs // 3, lambda n, _: update(3 * n, 3), 0)
+    lax.fori_loop(pairs // 3 * 3, pairs, lambda n, _: update(n, 1), 0)
     stores = []
     for target in range(GROUP):
         sums[target] = (-totals[target]).astype(sums.dtype)
@@ -205,7 +210,7 @@
         out_shape=(
             jax.ShapeDtypeStruct(diagonal.shape, jnp.float32),
             jax.ShapeDtypeStruct(panel.shape, jnp.bfloat16),
-            jax.ShapeDtypeStruct((GROUP, width, width), jnp.bfloat16),
+            jax.ShapeDtypeStruct((ROOM * GROUP, width, width), jnp.bfloat16),
             jax.ShapeDtypeStruct((8, 128), jnp.float32),
         ),
         in_specs=[smem, smem, vmem, hbm],
@@ -255,6 +260,8 @@
     last_recv,
     log_send,
     log_recv,
+    base,
+    base_sem,
 ):
     me = lax.axis_index("dev")
     width = updated.shape[0]
@@ -275,6 +282,8 @@
             device_id_type=pl.DeviceIdType.MESH,
         )
 
+    fetch = pltpu.make_async_copy(trailing, base, base_sem)
+    fetch.start()
     barrier = pltpu.get_barrier_semaphore()
     for bit in range(bits):
         pl.semaphore_signal(
@@ -312,8 +321,8 @@
         copy = remote(
             sums.at[to_y * 4 + to_x * 2 + 1 - core], landed.at[n], core_send.at[n], core_recv.at[n], 0
         )
-        copy.start()
         core_copies.append(copy)
+    core_copies[0].start()
     upper, lower = pl.ds(0, half), pl.ds(half, half)
     x_copies = [
         remote(partial.at[n, upper], cross.at[n, upper], cross_send.at[n], cross_recv.at[n], 1)
@@ -326,11 +335,17 @@
     for n in range(4):
         local_copies[n].wait()
         core_copies[n].wait_recv()
+        if n == 0:
+            core_copies[1].start()
+            core_copies[2].start()
+        if n == 1:
+            core_copies[3].start()
         total = kept[n].astype(jnp.float32) + landed[n].astype(jnp.float32)
         if n < 3:
             partial[n] = total.astype(jnp.bfloat16)
         else:
-            updated[...] = trailing[...] + total
+            fetch.wait()
+            updated[...] = base[...] + total
         if n < 2:
             x_copies[n].start()
         if n == 0 or n == 2:
@@ -370,7 +385,7 @@
             jax.ShapeDtypeStruct(trailing.shape, jnp.float32),
             jax.ShapeDtypeStruct(logterm.shape, jnp.float32),
         ),
-        in_specs=[pl.BlockSpec(memory_space=pl.ANY), vmem, vmem],
+        in_specs=[pl.BlockSpec(memory_space=pl.ANY), vmem, pl.BlockSpec(memory_space=pl.ANY)],
         out_specs=(vmem, vmem),
         scratch_shapes=[
             pltpu.VMEM((4, *block), jnp.bfloat16),
@@ -390,9 +405,11 @@
             dma((2,)),
             dma((bits,)),
             dma((bits,)),
+            pltpu.VMEM(block, jnp.float32),
+            dma,
         ],
         compiler_params=pltpu.CompilerParams(
-            collective_id=0, has_side_effects=True, vmem_limit_bytes=60 * 1024 * 1024
+            collective_id=0, has_side_effects=True, vmem_limit_bytes=32 * 1024 * 1024
         ),
         name="exchange",
     )(sums, logterm, trailing)

time: 73.3 us -> 66.4 us (0.906)
  Pallas kernels: 67.2 us -> 62.2 us
  local copies, waits for them, and re-layouts: 3.45 us -> 2.17 us
    pallas_call x1, Pallas kernels: 35.2 us -> 31.4 us  [exchange(): pl.pallas_call(functools.partial(exchange_kernel, count, 1.0 / (count * w...]
    pallas_call x1, Pallas kernels: 32 us -> 30.8 us  [factor_and_update(): pl.pallas_call(factor_kernel, out_shape=(jax.ShapeDtypeStruct(diagonal.sh...]
    unnamed x1 -> x5, local copies, waits for them, and re-layouts: 2.26 us -> 1.66 us
where the time goes in v3:
time: 66.4 us; the launch traced here: 65.8 us
  Pallas kernels  62.2 us (94%)
  local copies, waits for them, and re-layouts  2.17 us (3%)
  between operations  1.41 us (2%)
    pallas_call x1, Pallas kernels, exchange(): pl.pallas_call(functools.partial(exchange_kernel, count, 1.0 / (count * w...  31.4 us
    pallas_call x1, Pallas kernels, factor_and_update(): pl.pallas_call(factor_kernel, out_shape=(jax.ShapeDtypeStruct(diagonal.sh...  30.8 us
    unnamed x5, local copies, waits for them, and re-layouts  1.66 us

profile of v3, /device:TPU:0, one launch (start us, length us, event | category | flops | bytes accessed | tf_op | source)
XLA Modules:
  0.0 65.8 jit_solution(14913204634528041692)
XLA Ops:
  0.6 0.0 copy-start
  1.4 30.8 %factor_and_update.1 = (f32[512,512]{1,0:T(8,128)}, bf16[3072,512]{1,0:T(8,128)(2,1)}, bf16[64,512,512]{2,1,0:T(8,128)(2,1)}, f32[8,128]{1,0:T(8,128)}) custom-call(s32[1]{0:T(128)S(6)} %copy.10.counts, s32[1,21]{1,0:T(1,128)} %targets.1, f32[512,512]{1,0:T(8,128)} %diagonal.1, bf16[3072,512]{1,0:T(8,128)(2,1)} %panel_source.1), custom_call_target="tpu_custom_call" | custom-call | tf_op jit(solution)/shard_map/factor_and_update/pallas_call | solution.py:208
  32.1 0.0 copy-done
  32.2 0.0 copy-start.1
  32.2 0.7 %copy-done.1 = f32[8,128]{1,0:T(8,128)S(1)} copy-done((f32[8,128]{1,0:T(8,128)S(1)}, f32[8,128]{1,0:T(8,128)}, u32[]{:S(2)}) %copy-start.1) | copy-done | bytes 4120
  32.9 31.4 %exchange.1 = (f32[512,512]{1,0:T(8,128)S(1)}, f32[8,128]{1,0:T(8,128)S(1)}) custom-call(bf16[64,512,512]{2,1,0:T(8,128)(2,1)} %get-tuple-element.12.sums, f32[8,128]{1,0:T(8,128)S(1)} %copy-done.1, f32[512,512]{1,0:T(8,128)S(1)} %copy-done), custom_call_target="tpu_custom_call" | custom-call | tf_op jit(solution)/shard_map/exchange/pallas_call | solution.py:382
  64.3 0.5 slice.3
  64.8 1.0 %copy.11 = f32[512,512]{1,0:T(8,128)} copy(f32[512,512]{1,0:T(8,128)S(1)} %get-tuple-element.22) | data formatting | bytes 2097152
Async XLA Ops:
  0.6 31.5 %copy-start = (f32[512,512]{1,0:T(8,128)S(1)}, f32[512,512]{1,0:T(8,128)}, u32[]{:S(2)}) copy-start(f32[512,512]{1,0:T(8,128)} %trailing.1) | copy-start | bytes 3145732
  32.2 0.7 %copy-start.1 = (f32[8,128]{1,0:T(8,128)S(1)}, f32[8,128]{1,0:T(8,128)}, u32[]{:S(2)}) copy-start(f32[8,128]{1,0:T(8,128)} %get-tuple-element.13.logterm) | copy-start | bytes 12292
